TPU v7x, 256 devices: a whole 4x4x8 slice. The times are simulated.
256 devices in a mesh: seq: 32 (over y, z), kvh: 8 (over x, core).
Axes of the slice: x: 4, y: 4, z: 8, core: 2. Of those that a mesh axis runs over, the one named last changes fastest.
Arguments:
- queries: bfloat16 [512, 8192], P(('seq', 'kvh')), may hold values from -47 to 47
- keys: bfloat16 [32768, 1024], P(('seq', 'kvh')), may hold values from -6 to 6
- omega: bfloat16 [32768, 4096], P('seq', 'kvh'), may hold values from -6 to 6
- block_offsets: int32 [4], replicated, may hold values from 0 to 255, as said below
Outputs:
- basis_out: float32 [512, 4096], P('seq', 'kvh')
- projection: float32 [4096, 32768], P('kvh', 'seq')
Inputs may be any that keep to these rules, and one draw needn't show every extreme that they name: `block_offsets`: block i lies in [i * s, (i + 1) * s) with s = 64; the first block is 0 and the last is 255.
All inputs are finite; a program needn't handle non-finite values.
Results may differ from a plain program's by a relative error of at most 0.012.
The roundings to bfloat16 on the way count: a program that leaves them out, or rounds other values in their place, can miss the bound.
Values may be sent and summed in bfloat16 or wider, within the bound.
A program may use at most 64 MiB of HBM per device.

v0:
```python
import math
import jax
import jax.numpy as jnp
from jax import lax
from jax.sharding import PartitionSpec as P

POWER = 2
QBLK = 128
very_negative = -1e30


def combined_all(value, axis, join):
    pieces = jax.tree.map(lambda part: lax.all_gather(part, axis), value)
    head = jax.tree.map(lambda part: part[0], pieces)
    tail = jax.tree.map(lambda part: part[1:], pieces)
    so_far, _ = lax.scan(lambda so_far, share: (join(so_far, share), None), head, tail)
    return so_far


def gram_matrix(sketch):
    return jnp.einsum(
        "ngr,ngs->grs",
        sketch,
        sketch,
        precision=lax.Precision.HIGHEST,
        preferred_element_type=jnp.float32,
    )


def apply_factor(sketch, gram_total):
    factor = jnp.linalg.cholesky(gram_total)
    solved = jax.scipy.linalg.solve_triangular(factor, jnp.transpose(sketch, (1, 2, 0)), lower=True)
    return jnp.transpose(solved, (2, 0, 1))


def merge_softmax(first_pair, second_pair):
    largest = jnp.maximum(first_pair[0], second_pair[0])
    total_sum = first_pair[1] * jnp.exp(first_pair[0] - largest) + second_pair[1] * jnp.exp(
        second_pair[0] - largest
    )
    return (largest, total_sum)


def unchanged(value):
    return value


def body(queries, keys, omega, block_offsets):
    seq_count = lax.axis_size("seq")
    seq_rank = lax.axis_index("seq")
    local_queries, local_keys = (
        lax.all_to_all(queries, "kvh", split_axis=1, concat_axis=0, tiled=True),
        lax.all_to_all(keys, "kvh", split_axis=1, concat_axis=0, tiled=True),
    )
    slab_rows = lax.all_gather(local_queries, "seq", axis=0, tiled=True)
    head_size = local_keys.shape[1]
    groups = local_queries.shape[1] // head_size
    sketch_width = omega.shape[1] // groups
    key_count = local_keys.shape[0]
    half_keys = key_count // 2
    query_total = slab_rows.shape[0]
    own_count = local_queries.shape[0]
    block_count = query_total // QBLK
    tile_count = 2 * block_count
    inverse_root = 1.0 / math.sqrt(head_size)
    query_blocks = slab_rows.reshape(block_count, QBLK, groups, head_size)
    key_halves = local_keys.reshape(2, half_keys, head_size)
    omega_halves = omega.reshape(2, half_keys, groups, sketch_width)
    first_start = seq_rank * key_count
    second_start = seq_rank * key_count + half_keys
    half_starts = jnp.stack([first_start, second_start])

    def is_active(block_index, half_index):
        offset = lax.dynamic_index_in_dim(block_offsets, block_index, 0, keepdims=False)
        key_start = lax.dynamic_index_in_dim(half_starts, half_index, 0, keepdims=False)
        return offset * QBLK + QBLK - 1 >= key_start

    def tile_scores(block_index, half_index):
        query_rows = lax.dynamic_index_in_dim(query_blocks, block_index, 0, keepdims=False)
        key_rows = lax.dynamic_index_in_dim(key_halves, half_index, 0, keepdims=False)
        scores = (
            jnp.einsum("qgd,kd->gqk", query_rows, key_rows, preferred_element_type=jnp.float32)
            * inverse_root
        )
        offset = lax.dynamic_index_in_dim(block_offsets, block_index, 0, keepdims=False)
        key_start = lax.dynamic_index_in_dim(half_starts, half_index, 0, keepdims=False)
        query_pos = offset * QBLK + jnp.arange(QBLK, dtype=jnp.int32)
        key_pos = key_start + jnp.arange(half_keys, dtype=jnp.int32)
        allowed = key_pos[None, :] <= query_pos[:, None]
        return (scores, allowed)

    def stats_tile(tile_index, running):
        block_index = tile_index // 2
        half_index = tile_index % 2

        def stats_update(running):
            maxima, totals = running
            scores, allowed = tile_scores(block_index, half_index)
            masked = jnp.where(allowed[None], scores, very_negative)
            row_start = block_index * QBLK
            old_max = lax.dynamic_slice_in_dim(maxima, row_start, QBLK, 1)
            old_total = lax.dynamic_slice_in_dim(totals, row_start, QBLK, 1)
            new_max = jnp.maximum(old_max, jnp.max(masked, axis=-1))
            weights = jnp.where(allowed[None], jnp.exp(scores - new_max[..., None]), 0.0)
            new_total = old_total * jnp.exp(old_max - new_max) + jnp.sum(weights, axis=-1)
            maxima = lax.dynamic_update_slice_in_dim(maxima, new_max, row_start, 1)
            totals = lax.dynamic_update_slice_in_dim(totals, new_total, row_start, 1)
            return (maxima, totals)

        return lax.cond(is_active(block_index, half_index), stats_update, unchanged, running)

    start_max = jnp.full((groups, query_total), very_negative, jnp.float32)
    start_total = jnp.zeros((groups, query_total), jnp.float32)
    maxima, totals = lax.fori_loop(0, tile_count, stats_tile, (start_max, start_total))
    maxima, totals = combined_all((maxima, totals), "seq", merge_softmax)

    def tile_weights(block_index, half_index):
        scores, allowed = tile_scores(block_index, half_index)
        row_start = block_index * QBLK
        largest = lax.dynamic_slice_in_dim(maxima, row_start, QBLK, 1)
        total_rows = lax.dynamic_slice_in_dim(totals, row_start, QBLK, 1)
        weights = jnp.where(
            allowed[None], jnp.exp(scores - largest[..., None]) / total_rows[..., None], 0.0
        )
        return weights.astype(jnp.bfloat16)

    def forward(sketch_keys):

        def forward_tile(tile_index, result):
            block_index = tile_index // 2
            half_index = tile_index % 2

            def forward_update(result):
                weights = tile_weights(block_index, half_index)
                columns = lax.dynamic_index_in_dim(sketch_keys, half_index, 0, keepdims=False)
                product = jnp.einsum(
                    "gqk,kgr->qgr", weights, columns, preferred_element_type=jnp.float32
                )
                row_start = block_index * QBLK
                previous = lax.dynamic_slice_in_dim(result, row_start, QBLK, 0)
                return lax.dynamic_update_slice_in_dim(result, previous + product, row_start, 0)

            return lax.cond(is_active(block_index, half_index), forward_update, unchanged, result)

        initial = jnp.zeros((query_total, groups, sketch_width), jnp.float32)
        return lax.fori_loop(0, tile_count, forward_tile, initial)

    def backward(slab_basis):

        def backward_tile(tile_index, result):
            block_index = tile_index // 2
            half_index = tile_index % 2

            def backward_update(result):
                weights = tile_weights(block_index, half_index)
                row_start = block_index * QBLK
                query_side = lax.dynamic_slice_in_dim(slab_basis, row_start, QBLK, 0)
                product = jnp.einsum(
                    "gqk,qgr->kgr", weights, query_side, preferred_element_type=jnp.float32
                )
                previous = lax.dynamic_index_in_dim(result, half_index, 0, keepdims=False)
                return lax.dynamic_update_index_in_dim(result, previous + product, half_index, 0)

            return lax.cond(is_active(block_index, half_index), backward_update, unchanged, result)

        initial = jnp.zeros((2, half_keys, groups, sketch_width), jnp.float32)
        return lax.fori_loop(0, tile_count, backward_tile, initial)

    def range_basis(partial_value):
        flattened = partial_value.reshape(query_total, groups * sketch_width)
        owned = lax.psum_scatter(flattened, "seq", scatter_dimension=0, tiled=True).reshape(
            own_count, groups, sketch_width
        )
        gram_total = lax.psum(gram_matrix(owned), "seq")
        owned_basis = apply_factor(owned, gram_total)
        rounded = owned_basis.astype(jnp.bfloat16).reshape(own_count, groups * sketch_width)
        slab_basis = lax.all_gather(rounded, "seq", axis=0, tiled=True).reshape(
            query_total, groups, sketch_width
        )
        return (owned_basis, slab_basis)

    owned_basis, slab_basis = range_basis(forward(omega_halves))
    for power_step in range(POWER):
        key_side = backward(slab_basis).astype(jnp.bfloat16)
        owned_basis, slab_basis = range_basis(forward(key_side))
    projected = backward(slab_basis)
    key_total = key_count * seq_count
    projection = jnp.transpose(
        projected.reshape(key_count, groups, sketch_width), (1, 2, 0)
    ).reshape(groups * sketch_width, key_count) * math.sqrt(key_total)
    basis_out = owned_basis.reshape(own_count, groups * sketch_width) * math.sqrt(query_total)
    return (basis_out, projection)


def solution(mesh):
    placed = (P(("seq", "kvh"), None), P(("seq", "kvh"), None), P("seq", "kvh"), P())
    return jax.shard_map(
        body,
        mesh=mesh,
        in_specs=placed,
        out_specs=(P("seq", "kvh"), P("kvh", "seq")),
        check_vma=False,
    )
```

profile of v0, /device:TPU:2, one launch (start us, length us, event | category | flops | bytes accessed | tf_op | source)
XLA Modules:
  0.0 2066.3 jit_solution(2189012349922750271)
XLA Ops:
  7.2 9.6 all_to_all.35
  18.3 5.4 all-to-all-start
  28.8 66.4 %all-gather.4.cloned.1.call-done = bf16[512,1024]{1,0:T(8,128)(2,1)} async-done(((bf16[16,1024]{1,0:T(8,128)(2,1)}), bf16[512,1024]{1,0:T(8,128)(2,1)}) %all-gather.4.cloned.1.call-update) | async-done | bytes 1048592 | tf_op jit(solution)/shard_map/all_gather | solution.py:55
  98.0 56.3 %while.158 = (s32[]{:T(128)}, f32[8,512]{1,0:T(8,128)S(1)}, f32[8,512]{1,0:T(8,128)S(1)}, s32[4]{0:T(128)S(1)}, s32[2]{0:T(128)S(1)}, /*index=5*/bf16[2,512,128]...) while((s32[]{:T(128)}, f32[8,512]{1,0:T(8,128)S(1)}, ...), condition=%wide.region_5.6_spmd, body=%wide.region_0.5_spmd.sunk | while | flops 137956000 | bytes 4904592 | solution.py:114
  100.7 4.9 conditional.14
  111.1 4.9 conditional.14
  118.8 4.9 conditional.14
  126.4 4.9 conditional.14
  134.1 4.9 conditional.14
  141.7 4.9 conditional.14
  149.4 4.9 conditional.14
  154.3 46.2 %all-gather = f32[256,512]{1,0:T(8,128)S(1)} all-gather(f32[8,512]{1,0:T(8,128)S(1)} %get-tuple-element.2522), channel_id=2, replica_groups=mesh['seq'=32,'kvh'=8] {'seq'}, dimensions={0}, use_global_device_ids=true | all-gather | bytes 540672 | tf_op jit(solution)/shard_map/all_gather | solution.py:13
  200.5 49.5 %all-gather.1 = f32[256,512]{1,0:T(8,128)S(1)} all-gather(f32[8,512]{1,0:T(8,128)S(1)} %get-tuple-element.2523), channel_id=3, replica_groups=mesh['seq'=32,'kvh'=8] {'seq'}, dimensions={0}, use_global_device_ids=true | all-gather | bytes 540672 | tf_op jit(solution)/shard_map/all_gather | solution.py:13
  251.6 55.3 %while.160 = (s32[]{:T(128)}, f32[512,8,64]{0,2,1:T(8,128)S(1)}, s32[4]{0:T(128)S(1)}, s32[2]{0:T(128)S(1)}, bf16[2,512,8,64]{1,3,2,0:T(8,128)(2,1)S(1)}, /*inde...) while((s32[]{:T(128)}, f32[512,8,64]{0,2,1:T(8,128)S(1)}, ...), condition=%wide.region_11.12_spmd, body=%wide.region_8.11_spmd.sunk | while | flops 204079776 | bytes 1605252 | solution.py:146
  254.3 4.8 conditional.15
  264.6 4.8 conditional.15
  272.1 4.8 conditional.15
  279.6 4.8 conditional.15
  287.1 4.8 conditional.15
  294.6 4.8 conditional.15
  302.2 4.8 conditional.15
  308.3 208.1 %reduce-scatter.4.cloned.1.call-done = f32[16,512]{1,0:T(8,128)} async-done(((f32[512,512]{1,0:T(8,128)}), f32[16,512]{1,0:T(8,128)}) %reduce-scatter.4.cloned.1.call-update) | async-done | bytes 32784 | tf_op jit(solution)/shard_map/reduce_scatter | solution.py:171
  518.7 143.8 %all-reduce.4.cloned.1.call-done = f32[8,64,64]{1,2,0:T(8,128)} async-done(((f32[8,64,64]{1,2,0:T(8,128)}), f32[8,64,64]{1,2,0:T(8,128)}) %all-reduce.4.cloned.1.call-update) | async-done | bytes 131088 | tf_op jit(solution)/shard_map/psum | solution.py:174
  664.6 46.9 %custom-call.10 = f32[8,64,64]{2,1,0:T(8,128)S(1)} custom-call(f32[8,64,64]{2,1,0:T(8,128)S(1)} %fusion.182), custom_call_target="Cholesky" | custom-call | tf_op jit(solution)/shard_map/jit(cholesky)/cholesky | solution.py:31
  711.7 39.3 %custom-call.11 = f32[8,1,64,64]{2,3,1,0:T(8,128)S(1)} custom-call(f32[8,1,64,64]{3,2,1,0:T(8,128)S(1)} %select_bitcast_fusion.2), custom_call_target="InvertDiagBlocksLowerTriangular" | custom-call | tf_op jit(solution)/shard_map/jit(_solve_triangular)/vmap()/triangular_solve | solution.py:32
  751.5 48.3 %all_gather.29 = bf16[512,512]{1,0:T(8,128)(2,1)S(1)} all-gather(bf16[16,512]{1,0:T(8,128)(2,1)S(1)} %reshape.400), channel_id=1, replica_groups=mesh['seq'=32,'kvh'=8] {'seq'}, dimensions={0}, use_global_device_ids=true | all-gather | bytes 540672 | tf_op jit(solution)/shard_map/all_gather | solution.py:177
  801.1 55.4 %while.161 = (s32[]{:T(128)}, f32[2,512,8,64]{1,3,2,0:T(8,128)S(1)}, s32[4]{0:T(128)S(1)}, s32[2]{0:T(128)S(1)}, bf16[512,8,64]{0,2,1:T(8,128)(2,1)}, /*index=5*...) while((s32[]{:T(128)}, f32[2,512,8,64]{1,3,2,0:T(8,128)S(1)}, ...), condition=%wide.region_19.22_spmd, body=%wide.region_16.21_spmd.sunk | while | flops 204276384 | bytes 4882056 | solution.py:167
  803.7 4.9 conditional.16
  813.8 4.9 conditional.16
  821.4 4.9 conditional.16
  828.9 4.9 conditional.16
  836.5 4.9 conditional.16
  844.0 4.9 conditional.16
  851.6 4.9 conditional.16
  856.8 50.8 %while.162 = (s32[]{:T(128)}, f32[512,8,64]{0,2,1:T(8,128)S(1)}, s32[4]{0:T(128)S(1)}, s32[2]{0:T(128)S(1)}, bf16[2,512,8,64]{1,3,2,0:T(8,128)(2,1)S(1)}, /*inde...) while((s32[]{:T(128)}, f32[512,8,64]{0,2,1:T(8,128)S(1)}, ...), condition=%wide.region_23.26_spmd, body=%wide.region_20.25_spmd.sunk | while | flops 204079776 | bytes 1605252 | solution.py:146
  903.0 4.5 conditional.17
  908.9 208.1 %reduce-scatter.6.cloned.1.call-done = f32[16,512]{1,0:T(8,128)} async-done(((f32[512,512]{1,0:T(8,128)}), f32[16,512]{1,0:T(8,128)}) %reduce-scatter.6.cloned.1.call-update) | async-done | bytes 32784 | tf_op jit(solution)/shard_map/reduce_scatter | solution.py:171
  1119.3 143.7 %all-reduce.6.cloned.1.call-done = f32[8,64,64]{1,2,0:T(8,128)} async-done(((f32[8,64,64]{1,2,0:T(8,128)}), f32[8,64,64]{1,2,0:T(8,128)}) %all-reduce.6.cloned.1.call-update) | async-done | bytes 131088 | tf_op jit(solution)/shard_map/psum | solution.py:174
  1265.0 46.9 %custom-call.12 = f32[8,64,64]{2,1,0:T(8,128)S(1)} custom-call(f32[8,64,64]{2,1,0:T(8,128)S(1)} %fusion.180), custom_call_target="Cholesky" | custom-call | tf_op jit(solution)/shard_map/jit(cholesky)/cholesky | solution.py:31
  1312.2 39.3 %custom-call.13 = f32[8,1,64,64]{2,3,1,0:T(8,128)S(1)} custom-call(f32[8,1,64,64]{3,2,1,0:T(8,128)S(1)} %select_bitcast_fusion.1), custom_call_target="InvertDiagBlocksLowerTriangular" | custom-call | tf_op jit(solution)/shard_map/jit(_solve_triangular)/vmap()/triangular_solve | solution.py:32
  1352.0 48.1 %all_gather.30 = bf16[512,512]{1,0:T(8,128)(2,1)S(1)} all-gather(bf16[16,512]{1,0:T(8,128)(2,1)S(1)} %reshape.404), channel_id=1, replica_groups=mesh['seq'=32,'kvh'=8] {'seq'}, dimensions={0}, use_global_device_ids=true | all-gather | bytes 540672 | tf_op jit(solution)/shard_map/all_gather | solution.py:177
  1401.4 55.4 %while.163 = (s32[]{:T(128)}, f32[2,512,8,64]{1,3,2,0:T(8,128)S(1)}, s32[4]{0:T(128)S(1)}, s32[2]{0:T(128)S(1)}, bf16[512,8,64]{0,2,1:T(8,128)(2,1)}, /*index=5*...) while((s32[]{:T(128)}, f32[2,512,8,64]{1,3,2,0:T(8,128)S(1)}, ...), condition=%wide.region_29.32_spmd, body=%wide.region_26.31_spmd.sunk | while | flops 204276384 | bytes 4882056 | solution.py:167
  1404.0 4.9 conditional.18
  1414.1 4.9 conditional.18
  1421.7 4.9 conditional.18
  1429.2 4.9 conditional.18
  1436.8 4.9 conditional.18
  1444.3 4.9 conditional.18
  1451.8 4.9 conditional.18
  1457.1 50.8 %while.164 = (s32[]{:T(128)}, f32[512,8,64]{0,2,1:T(8,128)S(1)}, s32[4]{0:T(128)S(1)}, s32[2]{0:T(128)S(1)}, bf16[2,512,8,64]{1,3,2,0:T(8,128)(2,1)S(1)}, /*inde...) while((s32[]{:T(128)}, f32[512,8,64]{0,2,1:T(8,128)S(1)}, ...), condition=%wide.region_33.36_spmd, body=%wide.region_30.35_spmd.sunk | while | flops 204079776 | bytes 1605252 | solution.py:146
  1503.3 4.5 conditional.19
  1509.4 207.9 %reduce-scatter.8.cloned.1.call-done = f32[16,512]{1,0:T(8,128)} async-done(((f32[512,512]{1,0:T(8,128)}), f32[16,512]{1,0:T(8,128)}) %reduce-scatter.8.cloned.1.call-update) | async-done | bytes 32784 | tf_op jit(solution)/shard_map/reduce_scatter | solution.py:171
  1719.6 143.7 %all-reduce.8.cloned.1.call-done = f32[8,64,64]{1,2,0:T(8,128)} async-done(((f32[8,64,64]{1,2,0:T(8,128)}), f32[8,64,64]{1,2,0:T(8,128)}) %all-reduce.8.cloned.1.call-update) | async-done | bytes 131088 | tf_op jit(solution)/shard_map/psum | solution.py:174
  1865.3 46.9 %custom-call.14 = f32[8,64,64]{2,1,0:T(8,128)S(1)} custom-call(f32[8,64,64]{2,1,0:T(8,128)S(1)} %fusion.178), custom_call_target="Cholesky" | custom-call | tf_op jit(solution)/shard_map/jit(cholesky)/cholesky | solution.py:31
  1912.5 39.3 %custom-call.15 = f32[8,1,64,64]{2,3,1,0:T(8,128)S(1)} custom-call(f32[8,1,64,64]{3,2,1,0:T(8,128)S(1)} %select_bitcast_fusion), custom_call_target="InvertDiagBlocksLowerTriangular" | custom-call | tf_op jit(solution)/shard_map/jit(_solve_triangular)/vmap()/triangular_solve | solution.py:32
  1952.9 48.1 %all_gather.31 = bf16[512,512]{1,0:T(8,128)(2,1)S(1)} all-gather(bf16[16,512]{1,0:T(8,128)(2,1)S(1)} %reshape.408), channel_id=1, replica_groups=mesh['seq'=32,'kvh'=8] {'seq'}, dimensions={0}, use_global_device_ids=true | all-gather | bytes 540672 | tf_op jit(solution)/shard_map/all_gather | solution.py:177
  2002.3 54.7 %while.165 = (s32[]{:T(128)}, f32[2,512,8,64]{1,3,2,0:T(8,128)S(1)}, s32[4]{0:T(128)S(1)}, s32[2]{0:T(128)S(1)}, bf16[512,8,64]{0,2,1:T(8,128)(2,1)}, /*index=5*...) while((s32[]{:T(128)}, f32[2,512,8,64]{1,3,2,0:T(8,128)S(1)}, ...), condition=%wide.region_39.42_spmd, body=%wide.region_36.41_spmd.sunk | while | flops 204276384 | bytes 4882056 | solution.py:167
  2004.9 4.8 conditional.20
  2014.9 4.8 conditional.20
  2022.4 4.8 conditional.20
  2029.8 4.8 conditional.20
  2037.2 4.8 conditional.20
  2044.7 4.8 conditional.20
  2052.1 4.8 conditional.20
  (641 shorter events, 361.5 us)
Async XLA Ops:
  7.2 10.4 copy-start
  7.2 88.0 %all-gather.4.cloned.1.call-start = ((), (), s32[]{:S(2)}) async-start(), calls=%async_computation.5 | async-start | bytes 1081344 | tf_op jit(solution)/shard_map/all_gather | solution.py:55
  18.3 79.7 %all-to-all-start = ((bf16[128,8,128]{2,0,1:T(8,128)(2,1)}), bf16[128,8,128]{2,0,1:T(8,128)(2,1)}, u32[]{:S(2)}, u32[]{:S(2)}) async-start(bf16[128,8,128]{2,0,1:T(8,128)(2,1)} %copy_bitcast_fusion), calls=%async_computation | async-start | bytes 524288 | tf_op jit(solution)/shard_map/all_to_all | solution.py:53
  23.7 492.8 %reduce-scatter.4.cloned.1.call-start = ((), (), s32[]{:S(2)}) async-start(), calls=%async_computation.6 | async-start | bytes 1081344 | tf_op jit(solution)/shard_map/reduce_scatter | solution.py:171
  95.2 2.7 copy-start.3
  200.5 51.1 %copy-start.1 = (bf16[2,512,8,64]{1,3,2,0:T(8,128)(2,1)S(1)}, bf16[2,512,8,64]{1,3,2,0:T(8,128)(2,1)}, u32[]{:S(2)}) copy-start(bf16[2,512,8,64]{1,3,2,0:T(8,128)(2,1)} %copy.146) | copy-start | bytes 3145732
  308.3 354.2 %all-reduce.4.cloned.1.call-start = ((), (), s32[]{:S(2)}) async-start(), calls=%async_computation.7 | async-start | bytes 524288 | tf_op jit(solution)/shard_map/psum | solution.py:174
  518.6 598.5 %reduce-scatter.6.cloned.1.call-start = ((), (), s32[]{:S(2)}) async-start(), calls=%async_computation.8 | async-start | bytes 1081344 | tf_op jit(solution)/shard_map/reduce_scatter | solution.py:171
  908.9 354.1 %all-reduce.6.cloned.1.call-start = ((), (), s32[]{:S(2)}) async-start(), calls=%async_computation.9 | async-start | bytes 524288 | tf_op jit(solution)/shard_map/psum | solution.py:174
  1119.2 598.1 %reduce-scatter.8.cloned.1.call-start = ((), (), s32[]{:S(2)}) async-start(), calls=%async_computation.10 | async-start | bytes 1081344 | tf_op jit(solution)/shard_map/reduce_scatter | solution.py:171
  1509.2 354.1 %all-reduce.8.cloned.1.call-start = ((), (), s32[]{:S(2)}) async-start(), calls=%async_computation.11 | async-start | bytes 524288 | tf_op jit(solution)/shard_map/psum | solution.py:174
  2057.2 1.5 copy-start.2
Sparse Core Ops, SparseCore 0:
  17.6 77.5 all-gather.3
  308.4 207.9 reduce-scatter.3
  519.9 142.5 all-reduce.3
  909.0 208.0 reduce-scatter.5
  1120.4 142.5 all-reduce.5
  1509.3 208.0 reduce-scatter.7
  1720.8 142.3 all-reduce.7
where the time goes:
time: 2070 us
  waiting for transfers between devices  1120 us (54%)
  other arithmetic  306 us (15%)
  blocking collectives  250 us (12%)
  local copies, waits for them, and re-layouts  162 us (8%)
  loops' own time  110 us (5%)
  matrix products  96.3 us (5%)
    reduce_scatter x3, waiting for transfers between devices, range_basis(): lax.psum_scatter(flattened, 'seq', scatter_dimension=0, tiled=True)  624 us
    psum x3, waiting for transfers between devices, range_basis(): gram_total = lax.psum(gram_matrix(owned), 'seq')  431 us
    all_gather x3, blocking collectives, range_basis(): lax.all_gather(rounded, 'seq', axis=0, tiled=True)  144 us
    another operation x10, other arithmetic, apply_factor(): factor = jnp.linalg.cholesky(gram_total)  141 us
    another operation x7, other arithmetic, apply_factor(): jax.scipy.linalg.solve_triangular(factor, jnp.transpose(sketch, (1, 2, 0)...  118 us
    all_gather x2, blocking collectives, combined_all(): pieces = jax.tree.map(lambda part: lax.all_gather(part, axis), value)  95.6 us
    all_gather x1, waiting for transfers between devices, body(): slab_rows = lax.all_gather(local_queries, 'seq', axis=0, tiled=True)  66.4 us
    dot_general x21, matrix products, backward_update(): jnp.einsum('gqk,qgr->kgr', weights, query_side, preferred_element_type=jn...  41.8 us
  transfers between devices with their start and end apart: 8, of which 7 were waited for; matrix products, arithmetic and copies ran while one was open for 0% of the time, Pallas kernels for 0%

commit v1 on v0

--- a/solution.py
+++ b/solution.py
@@ -171,7 +171,7 @@
         owned = lax.psum_scatter(flattened, "seq", scatter_dimension=0, tiled=True).reshape(
             own_count, groups, sketch_width
         )
-        gram_total = lax.psum(gram_matrix(owned), "seq")
+        gram_total = jnp.sum(lax.all_gather(gram_matrix(owned), "seq"), axis=0)
         owned_basis = apply_factor(owned, gram_total)
         rounded = owned_basis.astype(jnp.bfloat16).reshape(own_count, groups * sketch_width)
         slab_basis = lax.all_gather(rounded, "seq", axis=0, tiled=True).reshape(

time: 2070 us -> 1930 us (0.932)
  waiting for transfers between devices: 1120 us -> 983 us
    psum x3 -> x0, waiting for transfers between devices: 431 us -> none  [range_basis(): gram_total = lax.psum(gram_matrix(owned), 'seq')]
    all_gather x0 -> x3, waiting for transfers between devices: none -> 291 us  [range_basis(): gram_total = jnp.sum(lax.all_gather(gram_matrix(owned), 'seq'), axis=0)]
where the time goes in v1:
time: 1930 us; the launch traced here: 1920 us
  waiting for transfers between devices  983 us (51%)
  other arithmetic  314 us (16%)
  blocking collectives  248 us (13%)
  local copies, waits for them, and re-layouts  155 us (8%)
  loops' own time  107 us (6%)
  matrix products  95.8 us (5%)
    reduce_scatter x3, waiting for transfers between devices, range_basis(): lax.psum_scatter(flattened, 'seq', scatter_dimension=0, tiled=True)  624 us
    all_gather x3, waiting for transfers between devices, range_basis(): gram_total = jnp.sum(lax.all_gather(gram_matrix(owned), 'seq'), axis=0)  291 us
    all_gather x3, blocking collectives, range_basis(): lax.all_gather(rounded, 'seq', axis=0, tiled=True)  143 us
    another operation x10, other arithmetic, apply_factor(): factor = jnp.linalg.cholesky(gram_total)  141 us
    another operation x7, other arithmetic, apply_factor(): jax.scipy.linalg.solve_triangular(factor, jnp.transpose(sketch, (1, 2, 0)...  118 us
    all_gather x2, blocking collectives, combined_all(): pieces = jax.tree.map(lambda part: lax.all_gather(part, axis), value)  95.5 us
    all_gather x1, waiting for transfers between devices, body(): slab_rows = lax.all_gather(local_queries, 'seq', axis=0, tiled=True)  67.2 us
    dot_general x21, matrix products, backward_update(): jnp.einsum('gqk,qgr->kgr', weights, query_side, preferred_element_type=jn...  41.8 us
  transfers between devices with their start and end apart: 8, of which 7 were waited for; matrix products, arithmetic and copies ran while one was open for 0% of the time, Pallas kernels for 0%

profile of v1, /device:TPU:2, one launch (start us, length us, event | category | flops | bytes accessed | tf_op | source)
XLA Modules:
  0.0 1923.2 jit_solution(1400725558340465868)
XLA Ops:
  7.2 9.6 all_to_all.35
  18.3 5.4 all-to-all-start
  28.0 67.2 %all-gather.10.cloned.1.call-done = bf16[512,1024]{1,0:T(8,128)(2,1)} async-done(((bf16[16,1024]{1,0:T(8,128)(2,1)}), bf16[512,1024]{1,0:T(8,128)(2,1)}) %all-gather.10.cloned.1.call-update) | async-done | bytes 1048592 | tf_op jit(solution)/shard_map/all_gather | solution.py:55
  97.9 56.2 %while.158 = (s32[]{:T(128)}, f32[8,512]{1,0:T(8,128)S(1)}, f32[8,512]{1,0:T(8,128)S(1)}, s32[4]{0:T(128)S(1)}, s32[2]{0:T(128)S(1)}, /*index=5*/bf16[2,512,128]...) while((s32[]{:T(128)}, f32[8,512]{1,0:T(8,128)S(1)}, ...), condition=%wide.region_5.6_spmd, body=%wide.region_0.5_spmd.sunk | while | flops 137956000 | bytes 4904592 | solution.py:114
  100.7 4.9 conditional.14
  111.1 4.9 conditional.14
  118.7 4.9 conditional.14
  126.3 4.9 conditional.14
  134.0 4.9 conditional.14
  141.6 4.9 conditional.14
  149.3 4.9 conditional.14
  154.2 46.2 %all-gather = f32[256,512]{1,0:T(8,128)S(1)} all-gather(f32[8,512]{1,0:T(8,128)S(1)} %get-tuple-element.2522), channel_id=2, replica_groups=mesh['seq'=32,'kvh'=8] {'seq'}, dimensions={0}, use_global_device_ids=true | all-gather | bytes 540672 | tf_op jit(solution)/shard_map/all_gather | solution.py:13
  200.4 49.3 %all-gather.1 = f32[256,512]{1,0:T(8,128)S(1)} all-gather(f32[8,512]{1,0:T(8,128)S(1)} %get-tuple-element.2523), channel_id=3, replica_groups=mesh['seq'=32,'kvh'=8] {'seq'}, dimensions={0}, use_global_device_ids=true | all-gather | bytes 540672 | tf_op jit(solution)/shard_map/all_gather | solution.py:13
  251.3 55.3 %while.160 = (s32[]{:T(128)}, f32[512,8,64]{0,2,1:T(8,128)S(1)}, s32[4]{0:T(128)S(1)}, s32[2]{0:T(128)S(1)}, bf16[2,512,8,64]{1,3,2,0:T(8,128)(2,1)S(1)}, /*inde...) while((s32[]{:T(128)}, f32[512,8,64]{0,2,1:T(8,128)S(1)}, ...), condition=%wide.region_11.12_spmd, body=%wide.region_8.11_spmd.sunk | while | flops 204079776 | bytes 1605252 | solution.py:146
  254.1 4.8 conditional.15
  264.3 4.8 conditional.15
  271.8 4.8 conditional.15
  279.3 4.8 conditional.15
  286.8 4.8 conditional.15
  294.3 4.8 conditional.15
  301.8 4.8 conditional.15
  308.0 208.1 %reduce-scatter.4.cloned.1.call-done = f32[16,512]{1,0:T(8,128)} async-done(((f32[512,512]{1,0:T(8,128)}), f32[16,512]{1,0:T(8,128)}) %reduce-scatter.4.cloned.1.call-update) | async-done | bytes 32784 | tf_op jit(solution)/shard_map/reduce_scatter | solution.py:171
  518.4 97.1 %all-gather.12.cloned.1.call-done = f32[256,64,64]{2,1,0:T(8,128)} async-done(((f32[8,64,64]{2,1,0:T(8,128)}), f32[256,64,64]{2,1,0:T(8,128)}) %all-gather.12.cloned.1.call-update) | async-done | bytes 4194320 | tf_op jit(solution)/shard_map/all_gather | solution.py:174
  615.6 4.4 reduce_sum.36
  620.1 46.9 %custom-call.10 = f32[8,64,64]{2,1,0:T(8,128)S(1)} custom-call(f32[8,64,64]{2,1,0:T(8,128)S(1)} %fusion.182), custom_call_target="Cholesky" | custom-call | tf_op jit(solution)/shard_map/jit(cholesky)/cholesky | solution.py:31
  667.3 39.3 %custom-call.11 = f32[8,1,64,64]{2,3,1,0:T(8,128)S(1)} custom-call(f32[8,1,64,64]{3,2,1,0:T(8,128)S(1)} %select_bitcast_fusion.2), custom_call_target="InvertDiagBlocksLowerTriangular" | custom-call | tf_op jit(solution)/shard_map/jit(_solve_triangular)/vmap()/triangular_solve | solution.py:32
  707.1 47.7 %all_gather.49 = bf16[512,512]{1,0:T(8,128)(2,1)S(1)} all-gather(bf16[16,512]{1,0:T(8,128)(2,1)S(1)} %reshape.400), channel_id=1, replica_groups=mesh['seq'=32,'kvh'=8] {'seq'}, dimensions={0}, use_global_device_ids=true | all-gather | bytes 540672 | tf_op jit(solution)/shard_map/all_gather | solution.py:177
  756.1 51.7 %while.161 = (s32[]{:T(128)}, f32[2,512,8,64]{1,3,2,0:T(8,128)S(1)}, s32[4]{0:T(128)S(1)}, s32[2]{0:T(128)S(1)}, bf16[512,8,64]{0,2,1:T(8,128)(2,1)}, /*index=5*...) while((s32[]{:T(128)}, f32[2,512,8,64]{1,3,2,0:T(8,128)S(1)}, ...), condition=%wide.region_19.22_spmd, body=%wide.region_16.21_spmd.sunk | while | flops 204276384 | bytes 4882056 | solution.py:167
  758.5 4.6 conditional.16
  768.0 4.6 conditional.16
  775.0 4.6 conditional.16
  782.1 4.6 conditional.16
  789.1 4.6 conditional.16
  796.1 4.6 conditional.16
  803.2 4.6 conditional.16
  808.1 50.7 %while.162 = (s32[]{:T(128)}, f32[512,8,64]{0,2,1:T(8,128)S(1)}, s32[4]{0:T(128)S(1)}, s32[2]{0:T(128)S(1)}, bf16[2,512,8,64]{1,3,2,0:T(8,128)(2,1)S(1)}, /*inde...) while((s32[]{:T(128)}, f32[512,8,64]{0,2,1:T(8,128)S(1)}, ...), condition=%wide.region_23.26_spmd, body=%wide.region_20.25_spmd.sunk | while | flops 204079776 | bytes 1605252 | solution.py:146
  860.2 208.1 %reduce-scatter.6.cloned.1.call-done = f32[16,512]{1,0:T(8,128)} async-done(((f32[512,512]{1,0:T(8,128)}), f32[16,512]{1,0:T(8,128)}) %reduce-scatter.6.cloned.1.call-update) | async-done | bytes 32784 | tf_op jit(solution)/shard_map/reduce_scatter | solution.py:171
  1070.5 97.1 %all-gather.14.cloned.1.call-done = f32[256,64,64]{2,1,0:T(8,128)} async-done(((f32[8,64,64]{2,1,0:T(8,128)}), f32[256,64,64]{2,1,0:T(8,128)}) %all-gather.14.cloned.1.call-update) | async-done | bytes 4194320 | tf_op jit(solution)/shard_map/all_gather | solution.py:174
  1167.6 4.4 reduce_sum.37
  1172.1 46.9 %custom-call.12 = f32[8,64,64]{2,1,0:T(8,128)S(1)} custom-call(f32[8,64,64]{2,1,0:T(8,128)S(1)} %fusion.180), custom_call_target="Cholesky" | custom-call | tf_op jit(solution)/shard_map/jit(cholesky)/cholesky | solution.py:31
  1219.3 39.3 %custom-call.13 = f32[8,1,64,64]{2,3,1,0:T(8,128)S(1)} custom-call(f32[8,1,64,64]{3,2,1,0:T(8,128)S(1)} %select_bitcast_fusion.1), custom_call_target="InvertDiagBlocksLowerTriangular" | custom-call | tf_op jit(solution)/shard_map/jit(_solve_triangular)/vmap()/triangular_solve | solution.py:32
  1259.1 47.5 %all_gather.52 = bf16[512,512]{1,0:T(8,128)(2,1)S(1)} all-gather(bf16[16,512]{1,0:T(8,128)(2,1)S(1)} %reshape.404), channel_id=1, replica_groups=mesh['seq'=32,'kvh'=8] {'seq'}, dimensions={0}, use_global_device_ids=true | all-gather | bytes 540672 | tf_op jit(solution)/shard_map/all_gather | solution.py:177
  1307.9 51.7 %while.163 = (s32[]{:T(128)}, f32[2,512,8,64]{1,3,2,0:T(8,128)S(1)}, s32[4]{0:T(128)S(1)}, s32[2]{0:T(128)S(1)}, bf16[512,8,64]{0,2,1:T(8,128)(2,1)}, /*index=5*...) while((s32[]{:T(128)}, f32[2,512,8,64]{1,3,2,0:T(8,128)S(1)}, ...), condition=%wide.region_29.32_spmd, body=%wide.region_26.31_spmd.sunk | while | flops 204276384 | bytes 4882056 | solution.py:167
  1310.3 4.6 conditional.18
  1319.8 4.6 conditional.18
  1326.8 4.6 conditional.18
  1333.9 4.6 conditional.18
  1340.9 4.6 conditional.18
  1348.0 4.6 conditional.18
  1355.0 4.6 conditional.18
  1359.9 50.7 %while.164 = (s32[]{:T(128)}, f32[512,8,64]{0,2,1:T(8,128)S(1)}, s32[4]{0:T(128)S(1)}, s32[2]{0:T(128)S(1)}, bf16[2,512,8,64]{1,3,2,0:T(8,128)(2,1)S(1)}, /*inde...) while((s32[]{:T(128)}, f32[512,8,64]{0,2,1:T(8,128)S(1)}, ...), condition=%wide.region_33.36_spmd, body=%wide.region_30.35_spmd.sunk | while | flops 204079776 | bytes 1605252 | solution.py:146
  1412.2 207.9 %reduce-scatter.8.cloned.1.call-done = f32[16,512]{1,0:T(8,128)} async-done(((f32[512,512]{1,0:T(8,128)}), f32[16,512]{1,0:T(8,128)}) %reduce-scatter.8.cloned.1.call-update) | async-done | bytes 32784 | tf_op jit(solution)/shard_map/reduce_scatter | solution.py:171
  1622.3 97.2 %all-gather.16.cloned.1.call-done = f32[256,64,64]{2,1,0:T(8,128)} async-done(((f32[8,64,64]{2,1,0:T(8,128)}), f32[256,64,64]{2,1,0:T(8,128)}) %all-gather.16.cloned.1.call-update) | async-done | bytes 4194320 | tf_op jit(solution)/shard_map/all_gather | solution.py:174
  1724.1 46.9 %custom-call.14 = f32[8,64,64]{2,1,0:T(8,128)S(1)} custom-call(f32[8,64,64]{2,1,0:T(8,128)S(1)} %fusion.178), custom_call_target="Cholesky" | custom-call | tf_op jit(solution)/shard_map/jit(cholesky)/cholesky | solution.py:31
  1771.3 39.3 %custom-call.15 = f32[8,1,64,64]{2,3,1,0:T(8,128)S(1)} custom-call(f32[8,1,64,64]{3,2,1,0:T(8,128)S(1)} %select_bitcast_fusion), custom_call_target="InvertDiagBlocksLowerTriangular" | custom-call | tf_op jit(solution)/shard_map/jit(_solve_triangular)/vmap()/triangular_solve | solution.py:32
  1811.1 47.5 %all_gather.55 = bf16[512,512]{1,0:T(8,128)(2,1)S(1)} all-gather(bf16[16,512]{1,0:T(8,128)(2,1)S(1)} %reshape.408), channel_id=1, replica_groups=mesh['seq'=32,'kvh'=8] {'seq'}, dimensions={0}, use_global_device_ids=true | all-gather | bytes 540672 | tf_op jit(solution)/shard_map/all_gather | solution.py:177
  1859.9 53.9 %while.165 = (s32[]{:T(128)}, f32[2,512,8,64]{1,3,2,0:T(8,128)S(1)}, s32[4]{0:T(128)S(1)}, s32[2]{0:T(128)S(1)}, bf16[512,8,64]{0,2,1:T(8,128)(2,1)}, /*index=5*...) while((s32[]{:T(128)}, f32[2,512,8,64]{1,3,2,0:T(8,128)S(1)}, ...), condition=%wide.region_39.42_spmd, body=%wide.region_36.41_spmd.sunk | while | flops 204276384 | bytes 4882056 | solution.py:167
  1862.4 4.8 conditional.20
  1872.3 4.8 conditional.20
  1879.6 4.8 conditional.20
  1886.9 4.8 conditional.20
  1894.3 4.8 conditional.20
  1901.6 4.8 conditional.20
  1909.0 4.8 conditional.20
  (642 shorter events, 360.3 us)
Async XLA Ops:
  7.2 10.4 copy-start
  7.2 88.0 %all-gather.10.cloned.1.call-start = ((), (), s32[]{:S(2)}) async-start(), calls=%async_computation.5 | async-start | bytes 1081344 | tf_op jit(solution)/shard_map/all_gather | solution.py:55
  18.3 79.6 %all-to-all-start = ((bf16[128,8,128]{2,0,1:T(8,128)(2,1)}), bf16[128,8,128]{2,0,1:T(8,128)(2,1)}, u32[]{:S(2)}, u32[]{:S(2)}) async-start(bf16[128,8,128]{2,0,1:T(8,128)(2,1)} %copy_bitcast_fusion), calls=%async_computation | async-start | bytes 524288 | tf_op jit(solution)/shard_map/all_to_all | solution.py:53
  23.7 492.5 %reduce-scatter.4.cloned.1.call-start = ((), (), s32[]{:S(2)}) async-start(), calls=%async_computation.6 | async-start | bytes 1081344 | tf_op jit(solution)/shard_map/reduce_scatter | solution.py:171
  95.2 2.7 copy-start.2
  308.0 307.6 %all-gather.12.cloned.1.call-start = ((), (), s32[]{:S(2)}) async-start(), calls=%async_computation.9 | async-start | bytes 8650752 | tf_op jit(solution)/shard_map/all_gather | solution.py:174
  518.3 549.9 %reduce-scatter.6.cloned.1.call-start = ((), (), s32[]{:S(2)}) async-start(), calls=%async_computation.7 | async-start | bytes 1081344 | tf_op jit(solution)/shard_map/reduce_scatter | solution.py:171
  860.1 307.4 %all-gather.14.cloned.1.call-start = ((), (), s32[]{:S(2)}) async-start(), calls=%async_computation.10 | async-start | bytes 8650752 | tf_op jit(solution)/shard_map/all_gather | solution.py:174
  1070.4 549.7 %reduce-scatter.8.cloned.1.call-start = ((), (), s32[]{:S(2)}) async-start(), calls=%async_computation.8 | async-start | bytes 1081344 | tf_op jit(solution)/shard_map/reduce_scatter | solution.py:171
  1412.0 307.6 %all-gather.16.cloned.1.call-start = ((), (), s32[]{:S(2)}) async-start(), calls=%async_computation.11 | async-start | bytes 8650752 | tf_op jit(solution)/shard_map/all_gather | solution.py:174
  1913.8 2.5 copy-start.1
Sparse Core Ops, SparseCore 0:
  17.6 77.5 all-gather.9
  308.1 208.0 reduce-scatter.3
  518.8 96.7 all-gather.11
  860.2 207.9 reduce-scatter.5
  1070.7 96.8 all-gather.13
  1412.1 207.9 reduce-scatter.7
  1622.7 96.7 all-gather.15
